TPU v7x, 256 devices: a whole 4x4x8 slice. The times are simulated.
256 devices in a mesh: train: 32 (over z_lo, y, core), task: 8 (over x, z_hi).
Axes of the slice: x: 4, y: 4, z: 8 (z_hi: 2, z_lo: 4; z = z_hi * 4 + z_lo), core: 2. Of those that a mesh axis runs over, the one named last changes fastest.
Arguments:
- train_grads: bfloat16 [1048576, 1024], P(('train', 'task')), may hold values from -6 to 6
- queries: bfloat16 [4096, 1024], P(('task', 'train')), may hold values from -6 to 6
- pair_blocks: int32 [4096, 4], P(('train', 'task')), may hold values from 0 to 31
- counts: int32 [4096], P(('train', 'task')), may hold values from 1 to 4, as said below
Outputs:
- scores: bfloat16 [4096, 4, 256, 128], P(('train', 'task'))
Inputs may be any that keep to these rules, and one draw needn't show every extreme that they name: `counts`: some train block has all 4 slots live.
All inputs are finite; a program needn't handle non-finite values.
Results may differ from a plain program's by a relative error of at most 0.002.
The roundings to bfloat16 on the way count: a program that leaves them out, or rounds other values in their place, can miss the bound.
Values may be sent and summed in bfloat16 or wider, within the bound.
A program may use at most 128 MiB of HBM per device.

v0:
```python
import math

import jax
import jax.numpy as jnp
from jax import lax
from jax.sharding import PartitionSpec as P

TRB = 256
QROWS = 128


def per_device(train_grads, queries, pair_blocks, counts):
    proj_width = train_grads.shape[1]
    partial_value = jnp.dot(train_grads.T, train_grads, preferred_element_type=jnp.float32)
    row_total = lax.axis_size("train") * lax.axis_size("task") * train_grads.shape[0]
    summed = lax.psum(partial_value, ("train", "task"))
    fisher = summed / row_total + 0.1 * jnp.eye(proj_width, dtype=jnp.float32)
    factor = jnp.linalg.cholesky(fisher)
    half_solved = lax.linalg.triangular_solve(
        factor, queries.astype(jnp.float32), left_side=False, lower=True, transpose_a=True
    )
    precond = lax.linalg.triangular_solve(factor, half_solved, left_side=False, lower=True).astype(
        jnp.bfloat16
    )
    group_rows = lax.all_gather(precond, "train", axis=0, tiled=True)
    every_query = lax.all_gather(group_rows, "task", axis=0, tiled=True)
    task_blocks = every_query.reshape(-1, QROWS, proj_width)
    train_blocks = train_grads.reshape(-1, TRB, proj_width)
    chosen = jnp.take(task_blocks, pair_blocks, axis=0)
    values = jnp.einsum("btk,bsqk->bstq", train_blocks, chosen, preferred_element_type=jnp.float32)
    values = values * (1.0 / math.sqrt(proj_width))
    live_slots = lax.broadcasted_iota(jnp.int32, pair_blocks.shape, 1) < counts[:, None]
    return jnp.where(live_slots[:, :, None, None], values, 0.0).astype(jnp.bfloat16)


def solution(mesh):
    in_specs = (
        P(("train", "task"), None),
        P(("task", "train"), None),
        P(("train", "task"), None),
        P(("train", "task")),
    )
    out_specs = P(("train", "task"), None, None, None)
    return jax.shard_map(
        per_device, mesh=mesh, in_specs=in_specs, out_specs=out_specs, check_vma=False
    )
```

profile of v0, /device:TPU:1, one launch (start us, length us, event | category | flops | bytes accessed | tf_op | source)
XLA Modules:
  0.0 916.1 jit_solution(15134832628582544377)
XLA Ops:
  6.5 15.0 %fusion.104 = f32[1024,1024]{0,1:T(8,128)} fusion(bf16[4096,1024]{1,0:T(8,128)(2,1)} %param.4), kind=kOutput, calls=%fused_computation.228 | convolution fusion | flops 8589934592 | bytes 12582912 | tf_op jit(solution)/shard_map/dot_general | solution.py:14
  22.3 270.1 %all-reduce.3.cloned.1.call-done = f32[1024,1024]{0,1:T(8,128)} async-done(((f32[1024,1024]{0,1:T(8,128)}), f32[1024,1024]{0,1:T(8,128)}) %all-reduce.3.cloned.1.call-update) | async-done | bytes 4194320 | tf_op jit(solution)/shard_map/psum | solution.py:16
  309.8 11.7 %cholesky.222 = f32[128,128]{1,0:T(8,128)S(1)} custom-call(f32[128,128]{1,0:T(8,128)S(1)} %cholesky.577), custom_call_target="Cholesky" | custom-call | tf_op jit(solution)/shard_map/jit(cholesky)/cholesky | solution.py:18
  321.6 9.8 %custom-call.64 = f32[1,128,128]{1,2,0:T(8,128)S(1)} custom-call(f32[1,128,128]{2,1,0:T(8,128)S(1)} %get-tuple-element.44), custom_call_target="InvertDiagBlocksLowerTriangular" | custom-call | tf_op jit(solution)/shard_map/jit(cholesky)/cholesky | solution.py:18
  334.8 11.7 %cholesky.243 = f32[128,128]{1,0:T(8,128)S(1)} custom-call(f32[128,128]{1,0:T(8,128)S(1)} %cholesky.581), custom_call_target="Cholesky" | custom-call | tf_op jit(solution)/shard_map/jit(cholesky)/cholesky | solution.py:18
  346.8 9.8 %custom-call.65 = f32[1,128,128]{1,2,0:T(8,128)S(1)} custom-call(f32[1,128,128]{2,1,0:T(8,128)S(1)} %get-tuple-element.42), custom_call_target="InvertDiagBlocksLowerTriangular" | custom-call | tf_op jit(solution)/shard_map/jit(cholesky)/cholesky | solution.py:18
  362.1 11.7 %cholesky.466 = f32[128,128]{1,0:T(8,128)S(1)} custom-call(f32[128,128]{1,0:T(8,128)S(1)} %cholesky.586), custom_call_target="Cholesky" | custom-call | tf_op jit(solution)/shard_map/jit(cholesky)/cholesky | solution.py:18
  374.6 9.8 %custom-call.66 = f32[1,128,128]{1,2,0:T(8,128)S(1)} custom-call(f32[1,128,128]{2,1,0:T(8,128)S(1)} %get-tuple-element.40), custom_call_target="InvertDiagBlocksLowerTriangular" | custom-call | tf_op jit(solution)/shard_map/jit(cholesky)/cholesky | solution.py:18
  389.0 11.7 %cholesky.485 = f32[128,128]{1,0:T(8,128)S(1)} custom-call(f32[128,128]{1,0:T(8,128)S(1)} %cholesky.591), custom_call_target="Cholesky" | custom-call | tf_op jit(solution)/shard_map/jit(cholesky)/cholesky | solution.py:18
  401.5 9.8 %custom-call.67 = f32[1,128,128]{1,2,0:T(8,128)S(1)} custom-call(f32[1,128,128]{2,1,0:T(8,128)S(1)} %get-tuple-element.38), custom_call_target="InvertDiagBlocksLowerTriangular" | custom-call | tf_op jit(solution)/shard_map/jit(cholesky)/cholesky | solution.py:18
  415.6 12.1 %cholesky.504 = f32[128,128]{1,0:T(8,128)S(1)} custom-call(f32[128,128]{1,0:T(8,128)S(1)} %cholesky.596), custom_call_target="Cholesky" | custom-call | tf_op jit(solution)/shard_map/jit(cholesky)/cholesky | solution.py:18
  428.5 9.8 %custom-call.68 = f32[1,128,128]{1,2,0:T(8,128)S(1)} custom-call(f32[1,128,128]{2,1,0:T(8,128)S(1)} %get-tuple-element.36), custom_call_target="InvertDiagBlocksLowerTriangular" | custom-call | tf_op jit(solution)/shard_map/jit(cholesky)/cholesky | solution.py:18
  442.5 11.7 %cholesky.524 = f32[128,128]{1,0:T(8,128)S(1)} custom-call(f32[128,128]{1,0:T(8,128)S(1)} %cholesky.601), custom_call_target="Cholesky" | custom-call | tf_op jit(solution)/shard_map/jit(cholesky)/cholesky | solution.py:18
  455.0 9.8 %custom-call.69 = f32[1,128,128]{1,2,0:T(8,128)S(1)} custom-call(f32[1,128,128]{2,1,0:T(8,128)S(1)} %get-tuple-element.34), custom_call_target="InvertDiagBlocksLowerTriangular" | custom-call | tf_op jit(solution)/shard_map/jit(cholesky)/cholesky | solution.py:18
  468.6 11.7 %cholesky.544 = f32[128,128]{1,0:T(8,128)S(1)} custom-call(f32[128,128]{1,0:T(8,128)S(1)} %cholesky.606), custom_call_target="Cholesky" | custom-call | tf_op jit(solution)/shard_map/jit(cholesky)/cholesky | solution.py:18
  481.1 9.8 %custom-call.70 = f32[1,128,128]{1,2,0:T(8,128)S(1)} custom-call(f32[1,128,128]{2,1,0:T(8,128)S(1)} %get-tuple-element.32), custom_call_target="InvertDiagBlocksLowerTriangular" | custom-call | tf_op jit(solution)/shard_map/jit(cholesky)/cholesky | solution.py:18
  494.1 11.7 %cholesky.562 = f32[128,128]{1,0:T(8,128)S(1)} custom-call(f32[128,128]{1,0:T(8,128)S(1)} %convolution_subtract_fusion.6), custom_call_target="Cholesky" | custom-call | tf_op jit(solution)/shard_map/jit(cholesky)/cholesky | solution.py:18
  521.1 24.4 %while.1 = (s32[]{:T(128)}, f32[1024,1024]{0,1:T(8,128)}, s32[8,2]{0,1:T(2,128)S(1)}, f32[8,128,128]{2,1,0:T(8,128)S(1)}, s32[]{:T(128)}) while((s32[]{:T(128)}, f32[1024,1024]{0,1:T(8,128)}, s32[8,2]{0,1:T(2,128)S(1)}, f32[8,128,128]{2,1,0:T(8,128)S(1)}, s32[]{:T(128)}) %tuple.51), condition=%wide.while_cond, body=%wide.while_body.sunk | while | flops 2 | bytes 393321 | solution.py:19
  545.5 78.8 %custom-call.71 = f32[8,128,128]{1,2,0:T(8,128)S(1)} custom-call(f32[8,128,128]{2,1,0:T(8,128)S(1)} %get-tuple-element.12), custom_call_target="InvertDiagBlocksLowerTriangular" | custom-call | tf_op jit(solution)/shard_map/triangular_solve | solution.py:19
  645.9 59.7 %all-gather.3.cloned.1.call-done = bf16[512,1024]{1,0:T(8,128)(2,1)} async-done(((bf16[16,1024]{1,0:T(8,128)(2,1)}), bf16[512,1024]{1,0:T(8,128)(2,1)}) %all-gather.3.cloned.1.call-update) | async-done | bytes 1048592 | tf_op jit(solution)/shard_map/all_gather | solution.py:25
  706.0 174.0 %all-gather.5.cloned.1.call-done = bf16[4096,1024]{1,0:T(8,128)(2,1)} async-done(((bf16[512,1024]{1,0:T(8,128)(2,1)}), bf16[4096,1024]{1,0:T(8,128)(2,1)}) %all-gather.5.cloned.1.call-update) | async-done | bytes 8388624 | tf_op jit(solution)/shard_map/all_gather | solution.py:26
  880.0 10.9 %gather_fusion = bf16[64,128,1024]{2,1,0:T(8,128)(2,1)} fusion(bf16[32,128,1024]{2,1,0:T(8,128)(2,1)} %bitcast.142, s32[1024]{0:T(1024)S(1)} %pad_clamp_fusion), kind=kCustom, calls=%fused_computation | custom fusion | bytes 33554688 | tf_op jit(solution)/shard_map/jit(_take)/gather | solution.py:29
  890.9 12.0 %fusion.4 = bf16[16,4,256,128]{2,3,1,0:T(8,128)(2,1)} fusion(pred[16,4]{1,0:T(8,128)(4,1)S(1)} %iota_compare_fusion.4, bf16[16,256,1024,1]{2,1,3,0:T(8,128)(2,1)} %bitcast.147, bf16[16,4,128,1024]{3,2,1,0:T(8,128)(2,1)} %bitcast.143, pred[16,4]{1,0:T(8,128)(4,1)S(1)} %copy.26), kind=kOutput, calls=%fused_computation.9 | convolution fusion | flops 4309647360 | bytes 29360256 | tf_op jit(solution)/shard_map/btk,bsqk->bstq/dot_general | solution.py:30
  902.9 6.4 copy.46
  (179 shorter events, 107.3 us)
Async XLA Ops:
  6.5 285.9 %all-reduce.3.cloned.1.call-start = ((), (), s32[]{:S(2)}) async-start(), calls=%async_computation | async-start | bytes 8388608 | tf_op jit(solution)/shard_map/psum | solution.py:16
  21.6 0.8 copy-start.2
  21.6 684.0 %all-gather.3.cloned.1.call-start = ((), (), s32[]{:S(2)}) async-start(), calls=%async_computation.1 | async-start | bytes 1081344 | tf_op jit(solution)/shard_map/all_gather | solution.py:25
  307.8 2.0 copy-start.1
  357.7 1.9 copy-start
  521.1 184.6 %copy-start.4 = (s32[16,4]{0,1:T(4,128)S(1)}, s32[16,4]{0,1:T(4,128)}, u32[]{:S(2)}) copy-start(s32[16,4]{0,1:T(4,128)} %param.6) | copy-start | bytes 772
  545.5 160.5 %copy-start.5 = (s32[16]{0:T(128)S(1)}, s32[16]{0:T(128)}, u32[]{:S(2)}) copy-start(s32[16]{0:T(128)} %param.7) | copy-start | bytes 196
  645.2 0.6 copy-start.3
  645.8 234.2 %all-gather.5.cloned.1.call-start = ((), (), s32[]{:S(2)}) async-start(), calls=%async_computation.2 | async-start | bytes 9437184 | tf_op jit(solution)/shard_map/all_gather | solution.py:26
Sparse Core Ops, SparseCore 0:
  21.7 270.7 all-reduce.2
  646.0 59.6 all-gather.2
  708.6 171.3 all-gather.4
where the time goes:
time: 922 us; the launch traced here: 916 us
  waiting for transfers between devices  504 us (55%)
  other arithmetic  261 us (28%)
  matrix products  73.5 us (8%)
  local copies, waits for them, and re-layouts  58.5 us (6%)
  between operations  18.9 us (2%)
    psum x1, waiting for transfers between devices, per_device(): summed = lax.psum(partial_value, ('train', 'task'))  270 us
    all_gather x1, waiting for transfers between devices, per_device(): every_query = lax.all_gather(group_rows, 'task', axis=0, tiled=True)  174 us
    another operation x30, other arithmetic, per_device(): factor = jnp.linalg.cholesky(fisher)  168 us
    another operation x3, other arithmetic, per_device(): lax.linalg.triangular_solve(factor, queries.astype(jnp.float32), left_sid...  83.7 us
    all_gather x1, waiting for transfers between devices, per_device(): group_rows = lax.all_gather(precond, 'train', axis=0, tiled=True)  59.7 us
    another operation x14, matrix products, per_device(): factor = jnp.linalg.cholesky(fisher)  26 us
    another operation x40, local copies, waits for them, and re-layouts  24.1 us
  transfers between devices with their start and end apart: 3, of which 3 were waited for; matrix products, arithmetic and copies ran while one was open for 0% of the time, Pallas kernels for 0%

commit v1 on v0

v1 whole, which is shorter than its diff:
```python
import functools
import math

import jax
import jax.numpy as jnp
from jax import lax
from jax.experimental import pallas as pl
from jax.experimental.pallas import tpu as pltpu
from jax.sharding import PartitionSpec as P

MESH = pl.DeviceIdType.MESH
TRB = 256
QROWS = 128
BLK = 128
NB = 8
DAMP = 0.1
TAU = 1e-5
PAIRS = [(i, j) for i in range(NB) for j in range(i + 1)]
SLOT = {pair: n for n, pair in enumerate(PAIRS)}
VMEM_LIMIT = 56 * 1024 * 1024


def coords():
    t, k = lax.axis_index("train"), lax.axis_index("task")
    core, y, x = lax.rem(t, 2), lax.rem(t // 2, 4), k // 2
    z = lax.rem(k, 2) * 4 + t // 8
    return core, x, y, z


def device(core, x, y, z):
    return ((lax.rem(z, 4) * 4 + y) * 2 + core, x * 2 + z // 4)


def meet(peers):
    barrier = pltpu.get_barrier_semaphore()
    for peer in peers:
        pl.semaphore_signal(barrier, inc=1, device_id=peer, device_id_type=MESH)
    pl.semaphore_wait(barrier, len(peers))


def gram_kernel(t_ref, out_ref):
    first = pl.program_id(0) == 0

    @pl.when(first)
    def _():
        out_ref[...] = jnp.zeros_like(out_ref)

    for bi in range(NB // 2):
        for bj in range(bi + 1):
            part = lax.dot_general(
                t_ref[:, bi * 256:(bi + 1) * 256],
                t_ref[:, bj * 256:(bj + 1) * 256],
                (((0,), (0,)), ((), ())),
                preferred_element_type=jnp.float32,
            )
            for u in range(2):
                for v in range(2):
                    pair = (2 * bi + u, 2 * bj + v)
                    if pair in SLOT:
                        at = SLOT[pair] * BLK
                        out_ref[at:at + BLK, :] += part[u * BLK:(u + 1) * BLK, v * BLK:(v + 1) * BLK]


def local_gram(t):
    rows, width = t.shape
    step = 1024
    return pl.pallas_call(
        gram_kernel,
        grid=(rows // step,),
        in_specs=[pl.BlockSpec((step, width), lambda i: (i, 0))],
        out_specs=pl.BlockSpec((len(PAIRS) * BLK, BLK), lambda i: (0, 0)),
        out_shape=jax.ShapeDtypeStruct((len(PAIRS) * BLK, BLK), jnp.float32),
        compiler_params=pltpu.CompilerParams(vmem_limit_bytes=VMEM_LIMIT),
        name="local_gram",
    )(t)


ROWS = 72
ZROWS = 24


def sum_kernel(g_ref, out_ref, r0, s1, ra, s2, rb, s3, rz, fz, send, recv):
    core, x, y, z = coords()
    sibling = device(1 - core, x, y, z)

    def along(axis, d):
        if axis == 0:
            return device(core, lax.rem(x + d, 4), y, z)
        if axis == 1:
            return device(core, x, lax.rem(y + d, 4), z)
        return device(core, x, y, lax.rem(z + d, 8))

    meet([sibling] + [along(a, d) for a in (0, 1) for d in (1, 2, 3)] + [along(2, d) for d in range(1, 8)])
    count = [0]

    def start(src, dst, to):
        n = count[0]
        count[0] += 1
        copy = pltpu.make_async_remote_copy(
            src_ref=src, dst_ref=dst, send_sem=send.at[n], recv_sem=recv.at[n], device_id=to, device_id_type=MESH
        )
        copy.start()
        return copy

    me = (x, y)
    copy = start(g_ref.at[1 - core], r0, sibling)
    copy.wait()
    s1[...] = g_ref[core] + r0[...]
    copies = []
    for h in range(2):
        for d in (1, 2, 3):
            copies.append(start(s1.at[h, lax.rem(me[h] + d, 4)], ra.at[h, d - 1], along(h, d)))
    for copy in copies:
        copy.wait()
    for h in range(2):
        s2[h] = s1[h, me[h]] + ra[h, 0] + ra[h, 1] + ra[h, 2]
    copies = []
    for h in range(2):
        for d in (1, 2, 3):
            copies.append(start(s2.at[h, lax.rem(me[1 - h] + d, 4)], rb.at[h, d - 1], along(1 - h, d)))
    for copy in copies:
        copy.wait()
    for h in range(2):
        s3[h * ROWS:(h + 1) * ROWS, :] = s2[h, me[1 - h]] + rb[h, 0] + rb[h, 1] + rb[h, 2]
    s3[2 * ROWS:, :] = jnp.zeros((8 * ZROWS - 2 * ROWS, BLK), jnp.float32)
    copies = []
    for d in range(1, 8):
        at = pl.multiple_of(lax.rem(z + d, 8) * ZROWS, 8)
        copies.append(start(s3.at[pl.ds(at, ZROWS)], rz.at[d - 1], along(2, d)))
    for copy in copies:
        copy.wait()
    mine = pl.ds(pl.multiple_of(z * ZROWS, 8), ZROWS)
    total = s3[mine, :]
    for d in range(7):
        total += rz[d]
    fz[mine, :] = total
    copies = [start(fz.at[mine], fz.at[mine], along(2, d)) for d in range(1, 8)]
    for copy in copies:
        copy.wait()
    out_ref[core, 0, x, y] = fz[0:ROWS, :]
    out_ref[core, 1, y, x] = fz[ROWS:2 * ROWS, :]
    copies = []
    for h in range(2):
        piece = out_ref.at[core, h, me[h], me[1 - h]]
        for d in (1, 2, 3):
            copies.append(start(piece, piece, along(1 - h, d)))
    for copy in copies:
        copy.wait()
    copies = []
    for h in range(2):
        piece = out_ref.at[core, h, me[h]]
        for d in (1, 2, 3):
            copies.append(start(piece, piece, along(h, d)))
    for copy in copies:
        copy.wait()
    copy = start(out_ref.at[core], out_ref.at[core], sibling)
    copy.wait()


def sum_gram(packed):
    shape = (2, 2, 4, 4, ROWS, BLK)
    f32 = jnp.float32
    out = pl.pallas_call(
        sum_kernel,
        in_specs=[pl.BlockSpec(memory_space=pltpu.VMEM)],
        out_specs=pl.BlockSpec(memory_space=pltpu.VMEM),
        out_shape=jax.ShapeDtypeStruct(shape, f32),
        scratch_shapes=[
            pltpu.VMEM(shape[1:], f32),
            pltpu.VMEM(shape[1:], f32),
            pltpu.VMEM((2, 3, 4, ROWS, BLK), f32),
            pltpu.VMEM((2, 4, ROWS, BLK), f32),
            pltpu.VMEM((2, 3, ROWS, BLK), f32),
            pltpu.VMEM((8 * ZROWS, BLK), f32),
            pltpu.VMEM((7, ZROWS, BLK), f32),
            pltpu.VMEM((8 * ZROWS, BLK), f32),
            pltpu.SemaphoreType.DMA((40,)),
            pltpu.SemaphoreType.DMA((40,)),
        ],
        compiler_params=pltpu.CompilerParams(collective_id=0, has_side_effects=True, vmem_limit_bytes=VMEM_LIMIT),
        name="sum_gram",
    )(packed.reshape(shape))
    return out.reshape(-1, BLK)


def split(v):
    hi = v.astype(jnp.bfloat16)
    return hi, (v - hi.astype(jnp.float32)).astype(jnp.bfloat16)


def solve_kernel(total, most, g_ref, q_ref, out_ref, flag_ref, hi_ref, lo_ref, d_ref):
    width = q_ref.shape[1]
    eye = lax.broadcasted_iota(jnp.int32, (BLK, BLK), 0) == lax.broadcasted_iota(jnp.int32, (BLK, BLK), 1)
    square = jnp.zeros((BLK, BLK), jnp.float32)
    for i, j in PAIRS:
        at = SLOT[i, j] * BLK
        block = g_ref[at:at + BLK, :] * (1.0 / total)
        if i == j:
            d_ref[:, i * BLK:(i + 1) * BLK] = jnp.sum(jnp.where(eye, block, 0.0), axis=0, keepdims=True) + DAMP
            block = jnp.where(eye, 0.0, block)
            square += block * block
        else:
            square += 2.0 * block * block
        hi, lo = split(block)
        hi_ref[i * BLK:(i + 1) * BLK, j * BLK:(j + 1) * BLK] = hi
        lo_ref[i * BLK:(i + 1) * BLK, j * BLK:(j + 1) * BLK] = lo
        if i != j:
            hi, lo = split(block.T)
            hi_ref[j * BLK:(j + 1) * BLK, i * BLK:(i + 1) * BLK] = hi
            lo_ref[j * BLK:(j + 1) * BLK, i * BLK:(i + 1) * BLK] = lo
    size = jnp.sum(square)
    diag = d_ref[...]
    rows = q_ref.shape[0]

    def apply(v):
        hi, lo = split(v)
        both = jnp.dot(jnp.concatenate([hi, lo], axis=0), hi_ref[...], preferred_element_type=jnp.float32)
        low = jnp.dot(hi, lo_ref[...], preferred_element_type=jnp.float32)
        return v * diag + (both[:rows] + (both[rows:] + low))

    def dots(a, b):
        return jnp.sum(a * b, axis=1, keepdims=True)

    def unsolved(state):
        step, _, _, _, _, left = state
        return jnp.logical_and(step < most, left > 0.0)

    def advance(state):
        step, sol, res, way, rr, _ = state
        image = apply(way)
        bend = dots(way, image)
        alpha = jnp.where(bend > 0.0, rr / bend, 0.0)
        sol = sol + alpha * way
        res = res - alpha * image
        after = dots(res, res)
        beta = jnp.where(rr > 0.0, after / rr, 0.0)
        left = jnp.sum(jnp.where(after <= (DAMP * TAU) ** 2 * dots(sol, sol), 0.0, 1.0))
        return step + 1, sol, res, res + beta * way, after, left

    res = q_ref[...].astype(jnp.float32)
    state = (jnp.int32(0), jnp.zeros((rows, width), jnp.float32), res, res, dots(res, res), jnp.float32(1.0))
    _, sol, _, _, _, left = lax.while_loop(unsolved, advance, state)
    out_ref[...] = sol.astype(jnp.bfloat16)
    good = jnp.logical_and(left == 0.0, size <= 4.0)
    flag_ref[0, 0] = jnp.where(good, 1, 0).astype(jnp.int32)


def solve(packed, queries, total):
    rows, width = queries.shape
    return pl.pallas_call(
        functools.partial(solve_kernel, total, 48),
        in_specs=[pl.BlockSpec(memory_space=pltpu.VMEM)] * 2,
        out_specs=[pl.BlockSpec(memory_space=pltpu.VMEM), pl.BlockSpec(memory_space=pltpu.SMEM)],
        out_shape=[
            jax.ShapeDtypeStruct((rows, width), jnp.bfloat16),
            jax.ShapeDtypeStruct((1, 1), jnp.int32),
        ],
        scratch_shapes=[
            pltpu.VMEM((width, width), jnp.bfloat16),
            pltpu.VMEM((width, width), jnp.bfloat16),
            pltpu.VMEM((1, width), jnp.float32),
        ],
        compiler_params=pltpu.CompilerParams(vmem_limit_bytes=VMEM_LIMIT),
        name="solve_rows",
    )(packed, queries)


def solve_direct(packed, queries, total):
    width = queries.shape[1]
    blocks = packed.reshape(len(PAIRS), BLK, BLK)
    rows = []
    for i in range(NB):
        row = [blocks[SLOT[i, j]] if i >= j else blocks[SLOT[j, i]].T for j in range(NB)]
        rows.append(jnp.concatenate(row, axis=1))
    fisher = jnp.concatenate(rows, axis=0) / total + DAMP * jnp.eye(width, dtype=jnp.float32)
    factor = jnp.linalg.cholesky(fisher)
    half = lax.linalg.triangular_solve(
        factor, queries.astype(jnp.float32), left_side=False, lower=True, transpose_a=True
    )
    return lax.linalg.triangular_solve(factor, half, left_side=False, lower=True).astype(jnp.bfloat16)


def gather_kernel(p_ref, out_ref, send, recv, own_sem):
    core, x, y, z = coords()
    sibling = device(1 - core, x, y, z)

    def along(axis, d):
        if axis == 0:
            return device(core, lax.rem(x + d, 4), y, z)
        if axis == 1:
            return device(core, x, lax.rem(y + d, 4), z)
        return device(core, x, y, lax.rem(z + d, 8))

    meet([sibling] + [along(a, d) for a in (0, 1) for d in (1, 3)] + [along(2, d) for d in range(1, 8)])
    count = [0]

    def start(piece, to, src=None):
        n = count[0]
        count[0] += 1
        copy = pltpu.make_async_remote_copy(
            src_ref=piece if src is None else src,
            dst_ref=piece,
            send_sem=send.at[n],
            recv_sem=recv.at[n],
            device_id=to,
            device_id_type=MESH,
        )
        copy.start()
        return copy

    me = (x, y)
    home = out_ref.at[:, x, z, y, core]
    own = pltpu.make_async_copy(p_ref, home, own_sem)
    own.start()
    copies = [start(home, along(2, d), p_ref) for d in range(1, 8)]
    own.wait()
    for copy in copies:
        copy.wait()

    def second(h, v, zs):
        if h == 0:
            return out_ref.at[0, x, zs, lax.rem(v, 4), core]
        return out_ref.at[1, lax.rem(v, 4), zs, y, core]

    def first(h, v, zs):
        if h == 0:
            return out_ref.at[0, lax.rem(v, 4), zs, :, core]
        return out_ref.at[1, :, zs, lax.rem(v, 4), core]

    whole, low, high = pl.ds(0, 8), pl.ds(0, 4), pl.ds(4, 4)
    copies = []
    for h in range(2):
        piece = second(h, me[1 - h], whole)
        copies += [start(piece, along(1 - h, 1)), start(piece, along(1 - h, 3))]
    for copy in copies:
        copy.wait()
    copies = []
    for h in range(2):
        copies.append(start(second(h, me[1 - h] + 3, low), along(1 - h, 1)))
        copies.append(start(second(h, me[1 - h] + 1, high), along(1 - h, 3)))
    for copy in copies:
        copy.wait()
    copies, over = [], []
    for h in range(2):
        piece = first(h, me[h], whole)
        copies += [start(piece, along(h, 1)), start(piece, along(h, 3))]
        over.append(start(piece, sibling))
    for copy in copies:
        copy.wait()
    copies = []
    for h in range(2):
        copies.append(start(first(h, me[h] + 3, low), along(h, 1)))
        copies.append(start(first(h, me[h] + 1, high), along(h, 3)))
        over.append(start(first(h, me[h] + 3, whole), sibling))
        over.append(start(first(h, me[h] + 1, whole), sibling))
    for copy in copies:
        copy.wait()
    for h in range(2):
        over.append(start(first(h, me[h] + 2, whole), sibling))
    for copy in over:
        copy.wait()


def gather_queries(precond):
    rows, width = precond.shape
    halves = precond.reshape(rows, 2, width // 2).transpose(1, 0, 2)
    out = pl.pallas_call(
        gather_kernel,
        in_specs=[pl.BlockSpec(memory_space=pltpu.VMEM)],
        out_specs=pl.BlockSpec(memory_space=pl.ANY),
        out_shape=jax.ShapeDtypeStruct((2, 4, 8, 4, 2, rows, width // 2), jnp.bfloat16),
        scratch_shapes=[
            pltpu.SemaphoreType.DMA((40,)),
            pltpu.SemaphoreType.DMA((40,)),
            pltpu.SemaphoreType.DMA,
        ],
        compiler_params=pltpu.CompilerParams(collective_id=1, has_side_effects=True, vmem_limit_bytes=VMEM_LIMIT),
        name="gather_queries",
    )(halves)
    return out.reshape(2, 32, QROWS, width // 2)


def score_kernel(scale, pair_ref, count_ref, t_ref, p_ref, out_ref):
    b = pl.program_id(0)
    half = t_ref.shape[1] // 2
    nt = (((1,), (1,)), ((), ()))
    for s in range(out_ref.shape[1]):
        live = s < count_ref[b]

        @pl.when(live)
        def _():
            q = pair_ref[b * out_ref.shape[1] + s]
            value = lax.dot_general(t_ref[:, :half], p_ref[0, q], nt, preferred_element_type=jnp.float32)
            value += lax.dot_general(t_ref[:, half:], p_ref[1, q], nt, preferred_element_type=jnp.float32)
            out_ref[0, s] = (value * scale).astype(out_ref.dtype)

        @pl.when(jnp.logical_not(live))
        def _():
            out_ref[0, s] = jnp.zeros(out_ref.shape[2:], out_ref.dtype)


def score(t, queries, pair_blocks, counts):
    blocks, slots = pair_blocks.shape
    width = t.shape[1]
    return pl.pallas_call(
        functools.partial(score_kernel, 1.0 / math.sqrt(width)),
        grid_spec=pltpu.PrefetchScalarGridSpec(
            num_scalar_prefetch=2,
            grid=(blocks,),
            in_specs=[
                pl.BlockSpec((TRB, width), lambda b, *_: (b, 0)),
                pl.BlockSpec(queries.shape, lambda b, *_: (0, 0, 0, 0), pipeline_mode=pl.Buffered(1)),
            ],
            out_specs=pl.BlockSpec((1, slots, TRB, QROWS), lambda b, *_: (b, 0, 0, 0)),
        ),
        out_shape=jax.ShapeDtypeStruct((blocks, slots, TRB, QROWS), jnp.bfloat16),
        compiler_params=pltpu.CompilerParams(vmem_limit_bytes=VMEM_LIMIT),
        name="scores",
    )(pair_blocks.reshape(-1), counts, t, queries)


def per_device(train_grads, queries, pair_blocks, counts):
    total = lax.axis_size("train") * lax.axis_size("task") * train_grads.shape[0]
    packed = sum_gram(local_gram(train_grads))
    precond, flag = solve(packed, queries, total)
    precond = lax.cond(
        flag[0, 0] > 0,
        lambda p, g, q: p,
        lambda p, g, q: solve_direct(g, q, total),
        precond, packed, queries,
    )
    return score(train_grads, gather_queries(precond), pair_blocks, counts)


def solution(mesh):
    in_specs = (
        P(("train", "task"), None),
        P(("task", "train"), None),
        P(("train", "task"), None),
        P(("train", "task")),
    )
    out_specs = P(("train", "task"), None, None, None)
    return jax.shard_map(
        per_device, mesh=mesh, in_specs=in_specs, out_specs=out_specs, check_vma=False
    )
```

time: 922 us -> 582 us (0.63)
  waiting for transfers between devices: 504 us -> 0 us
  Pallas kernels: 0 us -> 139 us
  local copies, waits for them, and re-layouts: 58.5 us -> 115 us
  matrix products: 73.5 us -> 47.3 us
  between operations: 18.9 us -> 0.96 us
    psum x1 -> x0, waiting for transfers between devices: 270 us -> none  [per_device(): summed = lax.psum(partial_value, ('train', 'task'))]
    all_gather x2 -> x0, waiting for transfers between devices: 234 us -> none  [the longest x1 174 us: per_device(): every_query = lax.all_gather(group_rows, 'task', axis=0, tiled=True)]
    pallas_call x0 -> x5, Pallas kernels: none -> 139 us  [the longest x1 54.9 us: sum_gram(): pl.pallas_call(sum_kernel, in_specs=[pl.BlockSpec(memory_space=pltpu.VMEM...]
    cond x0 -> x124, local copies, waits for them, and re-layouts: none -> 61.4 us
    dot_general x2 -> x0, matrix products: 27 us -> none  [the longest x1 15 us: per_device(): jnp.dot(train_grads.T, train_grads, preferred_element_type=jnp.float32)]
    gather x1 -> x0, local copies, waits for them, and re-layouts: 10.9 us -> none  [per_device(): chosen = jnp.take(task_blocks, pair_blocks, axis=0)]
    another operation x34 -> x35, other arithmetic: 251 us -> 252 us  [the longest x31 169 us: solve_direct(): factor = jnp.linalg.cholesky(fisher)]
  transfers between devices with their start and end apart: 3 -> 0, of which waited for: 3 -> 0; matrix products, arithmetic and copies ran while one was open for 0% -> 0% of each run, Pallas kernels for 0% -> 0%
where the time goes in v1:
time: 582 us; the launch traced here: 571 us
  other arithmetic  262 us (45%)
  Pallas kernels  139 us (24%)
  local copies, waits for them, and re-layouts  115 us (20%)
  matrix products  47.3 us (8%)
  loops' own time  6.81 us (1%)
    another operation x31, other arithmetic, solve_direct(): factor = jnp.linalg.cholesky(fisher)  169 us
    another operation x3, other arithmetic, solve_direct(): lax.linalg.triangular_solve(factor, queries.astype(jnp.float32), left_sid...  83.7 us
    cond x124, local copies, waits for them, and re-layouts  61.4 us
    pallas_call x1, Pallas kernels, sum_gram(): pl.pallas_call(sum_kernel, in_specs=[pl.BlockSpec(memory_space=pltpu.VMEM...  54.9 us
    pallas_call x1, Pallas kernels, gather_queries(): pl.pallas_call(gather_kernel, in_specs=[pl.BlockSpec(memory_space=pltpu.V...  43.1 us
    another operation x14, matrix products, solve_direct(): factor = jnp.linalg.cholesky(fisher)  26.9 us
    another operation x40, local copies, waits for them, and re-layouts  24.1 us
    pallas_call x1, Pallas kernels, score(): pl.pallas_call(functools.partial(score_kernel, 1.0 / math.sqrt(width)), g...  21.1 us

profile of v1, /device:TPU:1, one launch (start us, length us, event | category | flops | bytes accessed | tf_op | source)
XLA Modules:
  0.0 571.4 jit_solution(16121554595483135227)
XLA Ops:
  1.3 9.6 %local_gram.1 = f32[4608,128]{1,0:T(8,128)} custom-call(bf16[4096,1024]{1,0:T(8,128)(2,1)} %t_ref.3), custom_call_target="tpu_custom_call" | custom-call | tf_op jit(solution)/shard_map/local_gram/pallas_call | solution.py:67
  10.9 54.9 %sum_gram.1 = f32[2,2,4,4,72,128]{5,4,3,2,1,0:T(8,128)S(1)} custom-call(f32[2,2,4,4,72,128]{5,4,3,2,1,0:T(8,128)} %bitcast.339), custom_call_target="tpu_custom_call" | custom-call | tf_op jit(solution)/shard_map/sum_gram/pallas_call | solution.py:163
  65.8 10.5 %solve_rows.1 = (bf16[16,1024]{1,0:T(8,128)(2,1)}, s32[1,1]{1,0:T(1,128)}) custom-call(f32[4608,128]{1,0:T(8,128)S(1)} %bitcast.313, bf16[16,1024]{1,0:T(8,128)(2,1)S(1)} %copy-done.14), custom_call_target="tpu_custom_call" | custom-call | tf_op jit(solution)/shard_map/solve_rows/pallas_call | solution.py:250
  77.0 428.5 %conditional.1 = (bf16[16,1024]{1,0:T(8,128)(2,1)}) conditional(s32[]{:T(128)} %bitcast.91, (f32[2,2,4,4,72,128]{5,4,3,2,1,0:T(8,128)S(1)}, bf16[16,1024]{1,0:T(8,128)(2,1)S(1)}) %tuple.92, bf16[16,1024]{1,0:T(8,128)(2,1)} %get-tuple-element.18), branch_computations={%region_0.17_spmd, %region_17.18_spmd} | conditional | flops 3060970752 | bytes 115053312 | solution.py:426
  153.2 5.8 %copy.91 = f32[1024,1024]{1,0:T(8,128)} copy(f32[1024,1024]{0,1:T(8,128)} %select_add_fusion) | data formatting | bytes 8388608 | tf_op jit(solution)/shard_map/cond/branch_0_fun/add | solution.py:275
  165.5 11.7 %cholesky.5 = f32[128,128]{1,0:T(8,128)S(1)} custom-call(f32[128,128]{1,0:T(8,128)S(1)} %cholesky.221), custom_call_target="Cholesky" | custom-call | tf_op jit(solution)/shard_map/cond/branch_0_fun/jit(cholesky)/cholesky | solution.py:276
  179.9 9.8 %custom-call.56 = f32[1,128,128]{1,2,0:T(8,128)S(1)} custom-call(f32[1,128,128]{2,1,0:T(8,128)S(1)} %get-tuple-element.92), custom_call_target="InvertDiagBlocksLowerTriangular" | custom-call | tf_op jit(solution)/shard_map/cond/branch_0_fun/jit(cholesky)/cholesky | solution.py:276
  193.8 11.8 %cholesky.27 = f32[128,128]{1,0:T(8,128)S(1)} custom-call(f32[128,128]{1,0:T(8,128)S(1)} %cholesky.227), custom_call_target="Cholesky" | custom-call | tf_op jit(solution)/shard_map/cond/branch_0_fun/jit(cholesky)/cholesky | solution.py:276
  206.4 9.8 %custom-call.57 = f32[1,128,128]{1,2,0:T(8,128)S(1)} custom-call(f32[1,128,128]{2,1,0:T(8,128)S(1)} %get-tuple-element.90), custom_call_target="InvertDiagBlocksLowerTriangular" | custom-call | tf_op jit(solution)/shard_map/cond/branch_0_fun/jit(cholesky)/cholesky | solution.py:276
  220.2 11.7 %cholesky.58 = f32[128,128]{1,0:T(8,128)S(1)} custom-call(f32[128,128]{1,0:T(8,128)S(1)} %cholesky.232), custom_call_target="Cholesky" | custom-call | tf_op jit(solution)/shard_map/cond/branch_0_fun/jit(cholesky)/cholesky | solution.py:276
  232.7 9.8 %custom-call.58 = f32[1,128,128]{1,2,0:T(8,128)S(1)} custom-call(f32[1,128,128]{2,1,0:T(8,128)S(1)} %get-tuple-element.88), custom_call_target="InvertDiagBlocksLowerTriangular" | custom-call | tf_op jit(solution)/shard_map/cond/branch_0_fun/jit(cholesky)/cholesky | solution.py:276
  247.1 11.7 %cholesky.87 = f32[128,128]{1,0:T(8,128)S(1)} custom-call(f32[128,128]{1,0:T(8,128)S(1)} %cholesky.237), custom_call_target="Cholesky" | custom-call | tf_op jit(solution)/shard_map/cond/branch_0_fun/jit(cholesky)/cholesky | solution.py:276
  259.6 9.8 %custom-call.59 = f32[1,128,128]{1,2,0:T(8,128)S(1)} custom-call(f32[1,128,128]{2,1,0:T(8,128)S(1)} %get-tuple-element.86), custom_call_target="InvertDiagBlocksLowerTriangular" | custom-call | tf_op jit(solution)/shard_map/cond/branch_0_fun/jit(cholesky)/cholesky | solution.py:276
  273.7 12.1 %cholesky.116 = f32[128,128]{1,0:T(8,128)S(1)} custom-call(f32[128,128]{1,0:T(8,128)S(1)} %cholesky.242), custom_call_target="Cholesky" | custom-call | tf_op jit(solution)/shard_map/cond/branch_0_fun/jit(cholesky)/cholesky | solution.py:276
  286.6 9.8 %custom-call.60 = f32[1,128,128]{1,2,0:T(8,128)S(1)} custom-call(f32[1,128,128]{2,1,0:T(8,128)S(1)} %get-tuple-element.84), custom_call_target="InvertDiagBlocksLowerTriangular" | custom-call | tf_op jit(solution)/shard_map/cond/branch_0_fun/jit(cholesky)/cholesky | solution.py:276
  300.6 11.7 %cholesky.146 = f32[128,128]{1,0:T(8,128)S(1)} custom-call(f32[128,128]{1,0:T(8,128)S(1)} %cholesky.249), custom_call_target="Cholesky" | custom-call | tf_op jit(solution)/shard_map/cond/branch_0_fun/jit(cholesky)/cholesky | solution.py:276
  313.1 9.8 %custom-call.61 = f32[1,128,128]{1,2,0:T(8,128)S(1)} custom-call(f32[1,128,128]{2,1,0:T(8,128)S(1)} %get-tuple-element.82), custom_call_target="InvertDiagBlocksLowerTriangular" | custom-call | tf_op jit(solution)/shard_map/cond/branch_0_fun/jit(cholesky)/cholesky | solution.py:276
  326.7 11.7 %cholesky.176 = f32[128,128]{1,0:T(8,128)S(1)} custom-call(f32[128,128]{1,0:T(8,128)S(1)} %cholesky.256), custom_call_target="Cholesky" | custom-call | tf_op jit(solution)/shard_map/cond/branch_0_fun/jit(cholesky)/cholesky | solution.py:276
  339.2 9.8 %custom-call.62 = f32[1,128,128]{1,2,0:T(8,128)S(1)} custom-call(f32[1,128,128]{2,1,0:T(8,128)S(1)} %get-tuple-element.80), custom_call_target="InvertDiagBlocksLowerTriangular" | custom-call | tf_op jit(solution)/shard_map/cond/branch_0_fun/jit(cholesky)/cholesky | solution.py:276
  352.0 11.7 %cholesky.204 = f32[128,128]{1,0:T(8,128)S(1)} custom-call(f32[128,128]{1,0:T(8,128)S(1)} %convolution_subtract_fusion.6), custom_call_target="Cholesky" | custom-call | tf_op jit(solution)/shard_map/cond/branch_0_fun/jit(cholesky)/cholesky | solution.py:276
  380.5 24.4 %while.1 = (s32[]{:T(128)}, f32[1024,1024]{0,1:T(8,128)}, s32[8,2]{0,1:T(2,128)S(1)}, f32[8,128,128]{2,1,0:T(8,128)S(1)}, s32[]{:T(128)}) while((s32[]{:T(128)}, f32[1024,1024]{0,1:T(8,128)}, s32[8,2]{0,1:T(2,128)S(1)}, f32[8,128,128]{2,1,0:T(8,128)S(1)}, s32[]{:T(128)}) %tuple.87), condition=%wide.while_cond, body=%wide.while_body.sunk | while | flops 2 | bytes 393329 | solution.py:277
  404.9 78.8 %custom-call.63 = f32[8,128,128]{1,2,0:T(8,128)S(1)} custom-call(f32[8,128,128]{2,1,0:T(8,128)S(1)} %get-tuple-element.26), custom_call_target="InvertDiagBlocksLowerTriangular" | custom-call | tf_op jit(solution)/shard_map/cond/branch_0_fun/triangular_solve | solution.py:277
  506.9 43.1 %gather_queries.1 = bf16[2,4,8,4,2,16,512]{6,5,4,3,2,1,0:T(8,128)(2,1)} custom-call(bf16[2,16,512]{2,1,0:T(8,128)(2,1)} %bitcast.343), custom_call_target="tpu_custom_call" | custom-call | tf_op jit(solution)/shard_map/gather_queries/pallas_call | solution.py:367
  550.0 21.1 %scores.1 = bf16[16,4,256,128]{3,2,1,0:T(8,128)(2,1)} custom-call(s32[64]{0:T(128)} %reshape.102.pair_ref, s32[16]{0:T(128)} %count_ref.1, bf16[4096,1024]{1,0:T(8,128)(2,1)} %t_ref.3, bf16[2,32,128,512]{3,2,1,0:T(8,128)(2,1)} %bitcast.312), custom_call_target="tpu_custom_call" | custom-call | tf_op jit(solution)/shard_map/scores/pallas_call | solution.py:405
  (287 shorter events, 177.0 us)
Async XLA Ops:
  10.9 54.9 %copy-start.14 = (bf16[16,1024]{1,0:T(8,128)(2,1)S(1)}, bf16[16,1024]{1,0:T(8,128)(2,1)}, u32[]{:S(2)}) copy-start(bf16[16,1024]{1,0:T(8,128)(2,1)} %q_ref.1) | copy-start | bytes 98308
  77.0 0.6 copy-start.15
  79.2 4.8 copy-start.10
  79.9 13.4 %copy-start.1 = (f32[128,1024]{1,0:T(8,128)}, f32[128,1024]{1,0:T(8,128)S(1)}, u32[]{:S(2)}) copy-start(f32[128,1024]{1,0:T(8,128)S(1)} %get-tuple-element.77) | copy-start | bytes 1572868 | tf_op jit(solution)/shard_map/cond
  85.0 7.4 %copy-start.4 = (f32[1,128,128]{1,2,0:T(8,128)}, f32[1,128,128]{1,2,0:T(8,128)S(1)}, u32[]{:S(2)}) copy-start(f32[1,128,128]{1,2,0:T(8,128)S(1)} %copy.119) | copy-start | bytes 196612 | tf_op jit(solution)/shard_map/cond
  104.5 2.3 copy-start.8
  107.7 2.3 copy-start.5
  110.9 0.6 copy-start.2
  123.9 2.2 copy-start.9
  127.0 0.6 copy-start.6
  130.3 13.8 %copy-start.3 = (f32[1,128,128]{1,2,0:T(8,128)S(1)}, f32[1,128,128]{1,2,0:T(8,128)}, u32[]{:S(2)}) copy-start(f32[1,128,128]{1,2,0:T(8,128)} %copy-done.2) | copy-start | bytes 196612 | tf_op jit(solution)/shard_map/cond
  130.3 14.4 %copy-start.12 = (f32[128,128]{1,0:T(8,128)S(1)}, f32[128,128]{1,0:T(8,128)}, u32[]{:S(2)}) copy-start(f32[128,128]{1,0:T(8,128)} %get-tuple-element.70) | copy-start | bytes 196612 | tf_op jit(solution)/shard_map/cond
  130.4 15.2 %copy-start.7 = (f32[1,128,128]{1,2,0:T(8,128)S(1)}, f32[1,128,128]{1,2,0:T(8,128)}, u32[]{:S(2)}) copy-start(f32[1,128,128]{1,2,0:T(8,128)} %copy-done.6) | copy-start | bytes 196612 | tf_op jit(solution)/shard_map/cond
  130.4 15.8 %copy-start.11 = (f32[128,128]{1,0:T(8,128)S(1)}, f32[128,128]{1,0:T(8,128)}, u32[]{:S(2)}) copy-start(f32[128,128]{1,0:T(8,128)} %get-tuple-element.64) | copy-start | bytes 196612 | tf_op jit(solution)/shard_map/cond
  130.4 17.2 %copy-start.13 = (f32[1,128,128]{2,1,0:T(8,128)S(1)}, f32[1,128,128]{2,1,0:T(8,128)}, u32[]{:S(2)}) copy-start(f32[1,128,128]{2,1,0:T(8,128)} %get-tuple-element.45) | copy-start | bytes 196612 | tf_op jit(solution)/shard_map/cond
  163.5 1.9 copy-start
  375.6 108.1 %copy-start.16 = (bf16[16,1024]{1,0:T(8,128)(2,1)S(1)}, bf16[16,1024]{1,0:T(8,128)(2,1)}, u32[]{:S(2)}) copy-start(bf16[16,1024]{1,0:T(8,128)(2,1)} %copy-done.15) | copy-start | bytes 98308 | tf_op jit(solution)/shard_map/cond
  504.7 0.6 copy-start.17
